TPU v7x, 128 devices: a whole 4x4x4 slice. The times are simulated.
128 devices in a mesh: arc: 8 (over x, core), par: 16 (over y, z).
Axes of the slice: x: 4, y: 4, z: 4, core: 2. Of those that a mesh axis runs over, the one named last changes fastest.
Arguments:
- observations: float32 [2048, 65536], P('arc', 'par'), may hold values from -18 to 18
- arc_mask: int32 [16, 512], P('arc', 'par'), may hold values 0 or 1
- panel_owner: int32 [2], replicated, may hold values from 0 to 255, as said below
Outputs:
- info_rows: float32 [512, 65536], P('arc', 'par')
Inputs may be any that keep to these rules, and one draw needn't show every extreme that they name: `panel_owner`: two different panel indices below 256; one of the two is always the last panel.
All inputs are finite; a program needn't handle non-finite values. No bound on the sum of `arc_mask` on one device may be relied on, other than what follows from the above.
Results may differ from a plain program's by a relative error of at most 0.002.
Values sent between devices are 32-bit elements; how exact they have to be, the bound alone decides.
A program may use at most 64 MiB of HBM per device.

v0:
```python
import math

import jax
import jax.numpy as jnp
from jax import lax
from jax.sharding import PartitionSpec as P

PANEL = 256
BLK = 128


def spread(array, axis, root):
    mine = lax.axis_index(axis) == root
    return lax.psum(jnp.where(mine, array, jnp.zeros_like(array)), axis)


def matmul_high(left, right):
    return jnp.dot(left, right, precision=lax.Precision.HIGHEST, preferred_element_type=jnp.float32)


def inner_high(left, right):
    return lax.dot_general(
        left,
        right,
        (((0,), (0,)), ((), ())),
        precision=lax.Precision.HIGHEST,
        preferred_element_type=jnp.float32,
    )


def cholesky_loop(gram):
    order = gram.shape[0]
    positions = lax.broadcasted_iota(jnp.int32, (order, 1), 0)

    def one_column(column, lower):
        lower_row = lax.dynamic_slice_in_dim(lower, column, 1, 0)
        gram_col = lax.dynamic_slice_in_dim(gram, column, 1, 1)
        values = gram_col - matmul_high(lower, lower_row.T)
        pivot = lax.dynamic_slice_in_dim(values, column, 1, 0)
        scaled = jnp.where(positions >= column, values / jnp.sqrt(pivot), 0.0)
        return lax.dynamic_update_slice_in_dim(lower, scaled, column, 1)

    return lax.fori_loop(0, order, one_column, jnp.zeros_like(gram))


def lower_inverse(lower):
    order = lower.shape[0]
    columns = lax.broadcasted_iota(jnp.int32, (1, order), 1)

    def one_row(index, inverse):
        lower_row = lax.dynamic_slice_in_dim(lower, index, 1, 0)
        diag_entry = lax.dynamic_slice_in_dim(lower_row, index, 1, 1)
        unit_row = jnp.where(columns == index, 1.0, 0.0).astype(jnp.float32)
        new_row = (unit_row - matmul_high(lower_row, inverse)) / diag_entry
        return lax.dynamic_update_slice_in_dim(inverse, new_row, index, 0)

    return lax.fori_loop(0, order, one_row, jnp.zeros_like(lower))


def share_panel(design, panel_index):
    col_count = design.shape[1]
    col_start = panel_index * PANEL
    owner_root = col_start // col_count
    offset = col_start - owner_root * col_count
    local_cols = lax.dynamic_slice_in_dim(design, offset, PANEL, 1)
    return spread(local_cols, "par", owner_root)


def own_rows(stacked):
    arc_count = lax.axis_size("arc")
    row_share = stacked.shape[0] // arc_count
    row_start = lax.axis_index("arc") * row_share
    return lax.dynamic_slice_in_dim(stacked, row_start, row_share, 0)


def shards(observations, arc_mask, panel_owner):
    row_count, col_count = observations.shape
    row_blocks, col_blocks = arc_mask.shape
    total_rows = row_count * lax.axis_size("arc")
    shaped = observations.reshape(row_blocks, BLK, col_blocks, BLK)
    masked = shaped * arc_mask.astype(jnp.float32)[:, None, :, None]
    design = masked.reshape(row_count, col_count) / math.sqrt(total_rows)
    rows_out = []
    for panel_turn in range(2):
        panel_cols = share_panel(design, panel_owner[panel_turn])
        gram_block, cross_sums = lax.psum(
            (inner_high(panel_cols, panel_cols), inner_high(panel_cols, design)), "arc"
        )
        inverse = lower_inverse(cholesky_loop(gram_block))
        factor = matmul_high(inverse, cross_sums)
        rows_out.append(factor)
        if panel_turn == 0:
            coefficients = matmul_high(inverse.T, factor)
            design = design - matmul_high(panel_cols, coefficients)
    return own_rows(jnp.concatenate(rows_out, 0))


def solution(mesh):
    return jax.shard_map(
        shards,
        mesh=mesh,
        in_specs=(P("arc", "par"), P("arc", "par"), P()),
        out_specs=P("arc", "par"),
        check_vma=False,
    )
```

profile of v0, /device:TPU:1, one launch (start us, length us, event | category | flops | bytes accessed | tf_op | source)
XLA Modules:
  0.0 2376.9 jit_solution(8174050808208383253)
XLA Ops:
  6.5 1.4 fusion.28
  9.9 1.6 copy-done.5
  11.5 4.1 fusion.24
  15.6 2.0 copy-done
  18.3 86.5 %all-reduce.7.cloned.1.call-done = f32[256,256]{1,0:T(8,128)} async-done(((f32[256,256]{1,0:T(8,128)}), f32[256,256]{1,0:T(8,128)}) %all-reduce.7.cloned.1.call-update) | async-done | bytes 262160 | tf_op jit(solution)/shard_map/psum | solution.py:14
  104.8 8.0 fusion.30
  112.8 1.3 fusion.29
  115.0 71.6 %all-reduce.13.cloned.1.call-done = (f32[256,256]{1,0:T(8,128)}, f32[256,4096]{1,0:T(8,128)}) async-done(((f32[256,256]{1,0:T(8,128)}, f32[256,4096]{1,0:T(8,128)}), (f32[256,256]{1,0:T(8,128)}, f32[256,4096]{1,0:T(8,128)})) %all-reduce.13.cloned.1.call-update) | async-done | bytes 4456464 | tf_op jit(solution)/shard_map/psum | solution.py:86
  186.6 1.1 copy.11
  187.7 602.1 %while.62 = (s32[]{:T(128)}, f32[256,256]{1,0:T(8,128)S(1)}, f32[256,256]{0,1:T(8,128)S(1)}, s32[]{:T(128)}, s32[]{:T(128)}) while((s32[]{:T(128)}, f32[256,256]{1,0:T(8,128)S(1)}, f32[256,256]{0,1:T(8,128)S(1)}, s32[]{:T(128)}, s32[]{:T(128)}) %tuple.138), condition=%wide.region_3.4_spmd.clone, body=%wide.region_2.3_spmd.clone.sunk | while | flops 787458 | bytes 272469 | solution.py:43
  789.8 393.8 %while.63 = (s32[]{:T(128)}, f32[256,256]{1,0:T(8,128)S(1)}, f32[256,256]{1,0:T(8,128)S(1)}, s32[]{:T(128)}, s32[]{:T(128)}, /*index=5*/s32[]{:T(128)}) while((s32[]{:T(128)}, f32[256,256]{1,0:T(8,128)S(1)}, f32[256,256]{1,0:T(8,128)S(1)}, s32[]{:T(128)}, s32[]{:T(128)}, /*index=5*/s32[]{:T(128)}) %tuple.141), condition=%wide.region_5.6_spmd.clone, body=%wide.region_4.5_spmd.clone.sunk | while | flops 787459 | bytes 270449 | solution.py:57
  1183.7 5.4 fusion.31
  1189.1 3.8 fusion.32
  1192.9 3.8 convolution_subtract_fusion
  1196.7 2.0 copy-done.4
  1199.7 84.9 %all-reduce.9.cloned.1.call-done = f32[256,256]{1,0:T(8,128)} async-done(((f32[256,256]{1,0:T(8,128)}), f32[256,256]{1,0:T(8,128)}) %all-reduce.9.cloned.1.call-update) | async-done | bytes 262160 | tf_op jit(solution)/shard_map/psum | solution.py:14
  1284.6 8.0 fusion.34
  1292.6 1.3 fusion.33
  1293.9 72.7 %all-reduce.11.cloned.1.call-done = (f32[256,256]{1,0:T(8,128)}, f32[256,4096]{1,0:T(8,128)}) async-done(((f32[256,256]{1,0:T(8,128)}, f32[256,4096]{1,0:T(8,128)}), (f32[256,256]{1,0:T(8,128)}, f32[256,4096]{1,0:T(8,128)})) %all-reduce.11.cloned.1.call-update) | async-done | bytes 4456464 | tf_op jit(solution)/shard_map/psum | solution.py:86
  1366.6 1.1 copy.12
  1367.7 602.1 %while.64 = (s32[]{:T(128)}, f32[256,256]{1,0:T(8,128)S(1)}, f32[256,256]{0,1:T(8,128)S(1)}, s32[]{:T(128)}, s32[]{:T(128)}) while((s32[]{:T(128)}, f32[256,256]{1,0:T(8,128)S(1)}, f32[256,256]{0,1:T(8,128)S(1)}, s32[]{:T(128)}, s32[]{:T(128)}) %tuple.144), condition=%wide.region_10.11_spmd.clone, body=%wide.region_9.10_spmd.clone.sunk | while | flops 787458 | bytes 272469 | solution.py:43
  1969.8 393.8 %while.65 = (s32[]{:T(128)}, f32[256,256]{1,0:T(8,128)S(1)}, f32[256,256]{1,0:T(8,128)S(1)}, s32[]{:T(128)}, s32[]{:T(128)}, /*index=5*/s32[]{:T(128)}) while((s32[]{:T(128)}, f32[256,256]{1,0:T(8,128)S(1)}, f32[256,256]{1,0:T(8,128)S(1)}, s32[]{:T(128)}, s32[]{:T(128)}, /*index=5*/s32[]{:T(128)}) %tuple.147), condition=%wide.region_12.13_spmd.clone, body=%wide.region_11.12_spmd.clone.sunk | while | flops 787459 | bytes 270449 | solution.py:57
  2363.7 5.6 fusion.35
  2369.3 1.1 fusion.25
  (5149 shorter events, 1960.7 us)
Async XLA Ops:
  6.5 98.3 %all-reduce.7.cloned.1.call-start = ((), (), s32[]{:S(2)}) async-start(), calls=%async_computation | async-start | bytes 524288 | tf_op jit(solution)/shard_map/psum | solution.py:14
  9.3 2.2 copy-start.5
  15.6 2.0 copy-start
  18.3 168.3 %all-reduce.13.cloned.1.call-start = ((), (), s32[]{:S(2)}) async-start(), calls=%async_computation.3 | async-start | bytes 8912896 | tf_op jit(solution)/shard_map/psum | solution.py:86
  104.8 8.0 copy-start.6
  114.2 1170.4 %all-reduce.9.cloned.1.call-start = ((), (), s32[]{:S(2)}) async-start(), calls=%async_computation.1 | async-start | bytes 524288 | tf_op jit(solution)/shard_map/psum | solution.py:14
  1189.1 3.8 copy-start.2
  1189.1 3.8 copy-start.1
  1196.7 2.0 copy-start.4
  1199.4 167.2 %all-reduce.11.cloned.1.call-start = ((), (), s32[]{:S(2)}) async-start(), calls=%async_computation.2 | async-start | bytes 8912896 | tf_op jit(solution)/shard_map/psum | solution.py:86
  1284.6 8.0 copy-start.7
  2363.7 5.6 copy-start.3
Sparse Core Ops, SparseCore 0:
  18.4 86.3 all-reduce.6
  114.3 72.2 all-reduce.12
  1199.5 84.9 all-reduce.8
  1294.0 72.5 all-reduce.10
where the time goes:
time: 2390 us; the launch traced here: 2380 us
  local copies, waits for them, and re-layouts  1070 us (45%)
  other arithmetic  675 us (28%)
  waiting for transfers between devices  316 us (13%)
  matrix products  270 us (11%)
  loops' own time  34.5 us (1%)
    select_n x512, other arithmetic, one_column(): scaled = jnp.where(positions >= column, values / jnp.sqrt(pivot), 0.0)  333 us
    sqrt x512, local copies, waits for them, and re-layouts, one_column(): scaled = jnp.where(positions >= column, values / jnp.sqrt(pivot), 0.0)  332 us
    div x512, other arithmetic, one_row(): new_row = (unit_row - matmul_high(lower_row, inverse)) / diag_entry  332 us
    dynamic_slice x512, local copies, waits for them, and re-layouts, one_row(): diag_entry = lax.dynamic_slice_in_dim(lower_row, index, 1, 1)  321 us
    dynamic_update_slice x512, local copies, waits for them, and re-layouts, one_column(): return lax.dynamic_update_slice_in_dim(lower, scaled, column, 1)  314 us
    dot_general x1028, matrix products, matmul_high(): jnp.dot(left, right, precision=lax.Precision.HIGHEST, preferred_element_t...  251 us
    psum x2, waiting for transfers between devices, spread(): return lax.psum(jnp.where(mine, array, jnp.zeros_like(array)), axis)  171 us
    psum x2, waiting for transfers between devices, shards(): lax.psum((inner_high(panel_cols, panel_cols), inner_high(panel_cols, desi...  144 us

commit v1 on v0

v1 whole, which is shorter than its diff:
```python
import math

import jax
import jax.numpy as jnp
from jax import lax
from jax.experimental import pallas as pl
from jax.experimental.pallas import tpu as pltpu
from jax.sharding import PartitionSpec as P

PANEL = 256
BLK = 128
TILE = 128
HIGHEST = lax.Precision.HIGHEST


def dot_nt(left, right):
    return lax.dot_general(
        left, right, (((1,), (1,)), ((), ())), precision=HIGHEST, preferred_element_type=jnp.float32
    )


def dot_tn(left, right):
    return lax.dot_general(
        left, right, (((0,), (0,)), ((), ())), precision=HIGHEST, preferred_element_type=jnp.float32
    )


def dot_nn(left, right):
    return jnp.dot(left, right, precision=HIGHEST, preferred_element_type=jnp.float32)


def tile_inverse(tile, width=8):
    shape = (8, TILE)
    lanes = lax.broadcasted_iota(jnp.int32, shape, 1)
    subl = lax.broadcasted_iota(jnp.int32, shape, 0)
    count = TILE // 8
    rows = [tile[8 * i:8 * i + 8, :] for i in range(count)]
    for start in range(0, TILE, width):
        base = start // 8
        cols = [
            {i: jnp.broadcast_to(rows[i][:, start + c:start + c + 1], shape) for i in range(base, count)}
            for c in range(width)
        ]
        for c in range(width):
            col = start + c
            sub = col % 8
            pivot = jnp.broadcast_to(cols[c][base][sub:sub + 1, :], shape)
            inv = 1.0 / pivot
            prow = jnp.broadcast_to(rows[base][sub:sub + 1, :], shape) * inv
            prow = jnp.where(lanes == col, inv, prow)
            coef = {
                d: jnp.broadcast_to(cols[d][base][sub:sub + 1, :], shape) * inv for d in range(c + 1, width)
            }
            for i in range(base, count):
                if i == base and sub == 7:
                    continue
                mult = cols[c][i]
                keep = lanes == col
                if i == base:
                    mult = jnp.where(subl > sub, mult, 0.0)
                    keep = keep & (subl > sub)
                for d in range(c + 1, width):
                    cols[d][i] = cols[d][i] - mult * coef[d]
                rows[i] = jnp.where(keep, 0.0, rows[i]) - mult * prow
            rows[base] = jnp.where((lanes == col) & (subl == sub), pivot, rows[base])
    out = []
    for i in range(count):
        on_diag = lanes == subl + 8 * i
        diag = jnp.sum(jnp.where(on_diag, rows[i], 0.0), axis=1, keepdims=True)
        scaled = jnp.where(on_diag, 1.0, rows[i]) * lax.rsqrt(diag)
        out.append(jnp.where(lanes <= subl + 8 * i, scaled, 0.0))
    return jnp.concatenate(out, 0)


def factor_inverse(ref, order):
    count = order // TILE
    for k in range(count):
        low, top = k * TILE, (k + 1) * TILE
        inv = tile_inverse(ref[low:top, low:top])
        ref[low:top, low:top] = inv
        if k:
            ref[low:top, :low] = dot_nn(inv, ref[low:top, :low])
        if k + 1 < count:
            below = dot_nt(ref[top:, low:top], inv)
            for i in range(k + 1, count):
                part = below[(i - k - 1) * TILE:(i - k) * TILE]
                ref[i * TILE:(i + 1) * TILE, top:(i + 1) * TILE] -= dot_nt(part, below[:(i - k) * TILE])
            if k:
                ref[top:, :low] -= dot_nn(below, ref[low:top, :low])
            ref[top:, low:top] = -dot_nn(below, inv)
    for i in range(count - 1):
        ref[i * TILE:(i + 1) * TILE, (i + 1) * TILE:] = jnp.zeros((TILE, order - (i + 1) * TILE), jnp.float32)


def factor_kernel(gram_ref, out_ref):
    out_ref[...] = gram_ref[...]
    factor_inverse(out_ref, gram_ref.shape[0])


def factor_call(gram):
    return pl.pallas_call(
        factor_kernel,
        out_shape=jax.ShapeDtypeStruct(gram.shape, jnp.float32),
        compiler_params=pltpu.CompilerParams(vmem_limit_bytes=32 << 20),
        name="factor",
    )(gram)


def shards(observations, arc_mask, panel_owner):
    row_count, col_count = observations.shape
    row_blocks, col_blocks = arc_mask.shape
    total_rows = row_count * lax.axis_size("arc")
    shaped = observations.reshape(row_blocks, BLK, col_blocks, BLK)
    masked = shaped * arc_mask.astype(jnp.float32)[:, None, :, None]
    design = masked.reshape(row_count, col_count) / math.sqrt(total_rows)
    here = lax.axis_index("par")
    parts = []
    for turn in range(2):
        start = panel_owner[turn] * PANEL
        root = start // col_count
        local = lax.dynamic_slice_in_dim(design, start - root * col_count, PANEL, 1)
        parts.append(jnp.where(here == root, local, jnp.zeros_like(local)))
    panels = lax.psum(jnp.concatenate(parts, 1), "par")
    gram = lax.psum(dot_tn(panels, panels), "arc")
    weights = dot_nt(factor_call(gram), panels)
    return lax.psum_scatter(dot_nn(weights, design), "arc", scatter_dimension=0, tiled=True)


def solution(mesh):
    return jax.shard_map(
        shards,
        mesh=mesh,
        in_specs=(P("arc", "par"), P("arc", "par"), P()),
        out_specs=P("arc", "par"),
        check_vma=False,
    )
```

time: 2390 us -> 263 us (0.11)
  local copies, waits for them, and re-layouts: 1070 us -> 6.76 us
  other arithmetic: 675 us -> 5.69 us
  matrix products: 270 us -> 15 us
  waiting for transfers between devices: 316 us -> 202 us
  loops' own time: 34.5 us -> 0 us
    select_n x1026 -> x1, other arithmetic: 337 us -> 0.06 us  [shards(): parts.append(jnp.where(here == root, local, jnp.zeros_like(local)))]
    dynamic_update_slice x1024 -> x0, local copies, waits for them, and re-layouts: 336 us -> none  [the longest x512 314 us: one_column(): return lax.dynamic_update_slice_in_dim(lower, scaled, column, 1)]
    sqrt x512 -> x0, local copies, waits for them, and re-layouts: 332 us -> none  [one_column(): scaled = jnp.where(positions >= column, values / jnp.sqrt(pivot), 0.0)]
    div x512 -> x0, other arithmetic: 332 us -> none  [one_row(): new_row = (unit_row - matmul_high(lower_row, inverse)) / diag_entry]
    dynamic_slice x512 -> x0, local copies, waits for them, and re-layouts: 321 us -> none  [one_row(): diag_entry = lax.dynamic_slice_in_dim(lower_row, index, 1, 1)]
    dot_general x1032 -> x3, matrix products: 270 us -> 15 us  [the longest x1 10.7 us: dot_nn(): jnp.dot(left, right, precision=HIGHEST, preferred_element_type=jnp.float32)]
    psum x4 -> x2, waiting for transfers between devices: 316 us -> 148 us  [the longest x1 87.3 us: shards(): panels = lax.psum(jnp.concatenate(parts, 1), 'par')]
    select_n x512 -> x0, local copies, waits for them, and re-layouts: 68.2 us -> none  [one_column(): scaled = jnp.where(positions >= column, values / jnp.sqrt(pivot), 0.0)]
where the time goes in v1:
time: 263 us
  waiting for transfers between devices  202 us (77%)
  Pallas kernels  19.4 us (7%)
  matrix products  15 us (6%)
  between operations  14.6 us (6%)
  local copies, waits for them, and re-layouts  6.76 us (3%)
  other arithmetic  5.69 us (2%)
    psum x1, waiting for transfers between devices, shards(): panels = lax.psum(jnp.concatenate(parts, 1), 'par')  87.3 us
    psum x1, waiting for transfers between devices, shards(): gram = lax.psum(dot_tn(panels, panels), 'arc')  60.8 us
    reduce_scatter x1, waiting for transfers between devices, shards(): lax.psum_scatter(dot_nn(weights, design), 'arc', scatter_dimension=0, til...  53.4 us
    pallas_call x1, Pallas kernels, factor_call(): pl.pallas_call(factor_kernel, out_shape=jax.ShapeDtypeStruct(gram.shape,...  19.4 us
    dot_general x1, matrix products, dot_nn(): jnp.dot(left, right, precision=HIGHEST, preferred_element_type=jnp.float32)  10.7 us
  transfers between devices with their start and end apart: 3, of which 3 were waited for; matrix products, arithmetic and copies ran while one was open for 0% of the time, Pallas kernels for 0%

profile of v1, /device:TPU:1, one launch (start us, length us, event | category | flops | bytes accessed | tf_op | source)
XLA Modules:
  0.0 263.2 jit_solution(8961088715557240834)
XLA Ops:
  6.5 0.0 all-reduce.3.cloned.1.call-start
  6.5 1.4 fusion.1
  9.3 0.7 convert_element_type.3
  10.0 0.6 mul.31
  10.6 1.6 copy-done.3
  12.2 4.1 %fusion = f32[256,4096]{1,0:T(8,128)S(1)} fusion(f32[256,4096]{1,0:T(8,128)S(1)} %copy-done.3, f32[32,8,32,128]{3,2,1,0:T(8,128)S(1)} %bitcast.14), kind=kLoop, calls=%fused_computation.1 | loop fusion | flops 2097152 | bytes 12582912 | tf_op jit(solution)/shard_map/div | solution.py:115
  16.3 0.0 copy-start.1
  16.3 2.0 copy-done.1
  18.3 0.1 dynamic-slice_select_fusion.1
  18.3 0.9 pad_maximum_fusion
  19.2 0.0 all-reduce.3.cloned.1.call-update
  19.2 0.0 all-reduce.5.cloned.1.call-start
  19.3 87.3 %all-reduce.3.cloned.1.call-done = f32[256,512]{1,0:T(8,128)} async-done(((f32[256,512]{1,0:T(8,128)}), f32[256,512]{1,0:T(8,128)}) %all-reduce.3.cloned.1.call-update) | async-done | bytes 524304 | tf_op jit(solution)/shard_map/psum | solution.py:123
  106.6 3.3 %fusion.2 = f32[512,512]{1,0:T(8,128)} fusion(f32[256,512]{1,0:T(8,128)} %all-reduce.3.cloned.1.call-done), kind=kOutput, calls=%fused_computation.6 | convolution fusion | flops 805306368 | bytes 1572864 | tf_op jit(solution)/shard_map/dot_general | solution.py:23
  109.9 0.0 all-reduce.5.cloned.1.call-update
  109.9 0.2 reduce-scatter.2.cloned.1.call-start
  110.1 60.8 %all-reduce.5.cloned.1.call-done.gram_ref = f32[512,512]{1,0:T(8,128)} async-done(((f32[512,512]{1,0:T(8,128)}), f32[512,512]{1,0:T(8,128)}) %all-reduce.5.cloned.1.call-update) | async-done | bytes 1048592 | tf_op jit(solution)/shard_map/psum | solution.py:124
  170.9 1.2 copy-done
  172.2 19.4 %factor.1 = f32[512,512]{1,0:T(8,128)S(1)} custom-call(f32[512,512]{1,0:T(8,128)S(1)} %copy-done), custom_call_target="tpu_custom_call" | custom-call | tf_op jit(solution)/shard_map/factor/pallas_call | solution.py:101
  191.5 0.0 copy-done.2
  191.5 1.0 fusion.3
  192.6 10.7 %fusion.4 = f32[512,4096]{1,0:T(8,128)} fusion(f32[512,256]{1,0:T(8,128)S(1)} %fusion.3, f32[256,4096]{1,0:T(8,128)} %copy-done.1), kind=kOutput, calls=%fused_computation.8 | convolution fusion | flops 6442450944 | bytes 13107200 | tf_op jit(solution)/shard_map/dot_general | solution.py:29
  203.3 0.0 reduce-scatter.2.cloned.1.call-update
  203.3 53.4 %reduce-scatter.2.cloned.1.call-done = f32[64,4096]{1,0:T(8,128)} async-done(((f32[512,4096]{1,0:T(8,128)}), f32[64,4096]{1,0:T(8,128)}) %reduce-scatter.2.cloned.1.call-update) | async-done | bytes 1048592 | tf_op jit(solution)/shard_map/reduce_scatter | solution.py:126
  (3 shorter events, 0.0 us)
Async XLA Ops:
  6.5 100.1 %all-reduce.3.cloned.1.call-start = ((), (), s32[]{:S(2)}) async-start(), calls=%async_computation.1 | async-start | bytes 1048576 | tf_op jit(solution)/shard_map/psum | solution.py:123
  10.0 2.2 copy-start.3
  16.3 2.0 copy-start.1
  19.2 151.7 %all-reduce.5.cloned.1.call-start = ((), (), s32[]{:S(2)}) async-start(), calls=%async_computation.2 | async-start | bytes 2097152 | tf_op jit(solution)/shard_map/psum | solution.py:124
  106.6 84.9 %copy-start.2 = (f32[256,512]{1,0:T(8,128)S(1)}, f32[256,512]{1,0:T(8,128)}, u32[]{:S(2)}) copy-start(f32[256,512]{1,0:T(8,128)} %all-reduce.3.cloned.1.call-done) | copy-start | bytes 1572868
  109.9 146.8 %reduce-scatter.2.cloned.1.call-start = ((), (), s32[]{:S(2)}) async-start(), calls=%async_computation.3 | async-start | bytes 9437184 | tf_op jit(solution)/shard_map/reduce_scatter | solution.py:126
  170.9 1.2 copy-start
Sparse Core Ops, SparseCore 0:
  19.3 87.2 all-reduce.2
  110.0 60.8 all-reduce.4
  203.4 53.1 reduce-scatter.1

commit v2 on v0

v2 whole, which is shorter than its diff:
```python
import functools
import math

import jax
import jax.numpy as jnp
from jax import lax
from jax.experimental import pallas as pl
from jax.experimental.pallas import tpu as pltpu
from jax.sharding import PartitionSpec as P

PANEL = 256
BLK = 128
TILE = 128
HIGHEST = lax.Precision.HIGHEST
MESH = pl.DeviceIdType.MESH
F32 = jnp.float32
BF16 = jnp.bfloat16


def dot_nt(left, right):
    return lax.dot_general(left, right, (((1,), (1,)), ((), ())), precision=HIGHEST, preferred_element_type=F32)


def dot_nn(left, right):
    return jnp.dot(left, right, precision=HIGHEST, preferred_element_type=F32)


def halves(value):
    high = value.astype(BF16)
    return high, (value - high.astype(F32)).astype(BF16)


def tile_inverse(tile, width=8):
    lanes = lax.broadcasted_iota(jnp.int32, (8, TILE), 1)
    subl = lax.broadcasted_iota(jnp.int32, (8, TILE), 0)
    zero = jnp.zeros((8, TILE), F32)
    done = []
    tail = tile
    for start in range(0, TILE, width):
        base = start // 8
        size = TILE - 8 * base - 8
        head, tail = tail[:8], tail[8:]
        tail_lanes = lax.broadcasted_iota(jnp.int32, (size, TILE), 1) if size else None
        head_cols = [jnp.broadcast_to(head[:, start + c:start + c + 1], (8, TILE)) for c in range(width)]
        tail_cols = [jnp.broadcast_to(tail[:, start + c:start + c + 1], (size, TILE)) for c in range(width)] if size else None
        for c in range(width):
            col = start + c
            pivot = jnp.broadcast_to(head_cols[c][c:c + 1, :], (8, TILE))
            inv = 1.0 / pivot
            on_col = lanes == col
            prow = jnp.where(on_col, inv, jnp.broadcast_to(head[c:c + 1, :], (8, TILE)) * inv)
            below = subl > c
            mult = jnp.where(below, head_cols[c], zero)
            coefs = [jnp.broadcast_to(head_cols[d][c:c + 1, :], (8, TILE)) * inv for d in range(c + 1, width)]
            for d in range(c + 1, width):
                head_cols[d] = head_cols[d] - mult * coefs[d - c - 1]
            head = jnp.where(on_col, jnp.where(below, zero, jnp.where(subl == c, pivot, head)), head) - mult * prow
            if size:
                for d in range(c + 1, width):
                    tail_cols[d] = tail_cols[d] - tail_cols[c] * jnp.broadcast_to(coefs[d - c - 1][:1], (size, TILE))
                tail = jnp.where(tail_lanes == col, 0.0, tail) - tail_cols[c] * jnp.broadcast_to(prow[:1], (size, TILE))
        on_diag = lanes == subl + start
        diag = jnp.sum(jnp.where(on_diag, head, zero), axis=1, keepdims=True)
        scaled = jnp.where(on_diag, 1.0, head) * lax.rsqrt(diag)
        done.append(jnp.where(lanes <= subl + start, scaled, zero))
    return jnp.concatenate(done, 0)


def factor_step(ref, k, count):
    low, top = k * TILE, (k + 1) * TILE
    inv = tile_inverse(ref[low:top, low:top])
    ref[low:top, low:top] = inv
    if k:
        ref[low:top, :low] = dot_nn(inv, ref[low:top, :low])
    if k + 1 < count:
        below = dot_nt(ref[top:, low:top], inv)
        for i in range(k + 1, count):
            part = below[(i - k - 1) * TILE:(i - k) * TILE]
            ref[i * TILE:(i + 1) * TILE, top:(i + 1) * TILE] -= dot_nt(part, below[:(i - k) * TILE])
        if k:
            ref[top:, :low] -= dot_nn(below, ref[low:top, :low])
        ref[top:, low:top] = -dot_nn(below, inv)


def kernel(
    n_arc, n_par,
    obs_ref, mask_ref, owner_ref, out_ref,
    part_ref, piece_ref, panel_ref, stack_ref,
    gram_ref, gram_piece_ref, gram_all_ref, fac_ref,
    to_core_ref, from_core_ref, sums_ref, from_one_ref, from_two_ref, result_ref,
    part_sems, panel_sems, gram_sems, all_sems, fwd_sems, core_sems, one_sems, two_sems, out_sems,
):
    rows, cols = obs_ref.shape
    order = 2 * PANEL
    share = rows // n_par
    slice_rows = gram_piece_ref.shape[1]
    width = cols // 16
    out_rows = out_ref.shape[0]
    tiles = order // TILE
    chips = n_arc // 2
    scale = 1.0 / math.sqrt(rows * n_arc)
    arc = lax.axis_index("arc")
    par = lax.axis_index("par")
    chip = arc // 2
    core = arc % 2

    def send(src, dst, sems, slot, target):
        return pltpu.make_async_remote_copy(
            src_ref=src, dst_ref=dst, send_sem=sems.at[0, slot], recv_sem=sems.at[1, slot],
            device_id=target, device_id_type=MESH,
        )

    def each(count, body):
        lax.fori_loop(0, count, lambda i, carry: (body(i), carry)[1], 0)

    def par_peer(i):
        return lax.rem(par + i + 1, n_par)

    def arc_peer(i):
        return lax.rem(arc + i + 1, n_arc)

    barrier = pltpu.get_barrier_semaphore()
    each(n_par - 1, lambda i: pl.semaphore_signal(barrier, inc=1, device_id={"par": par_peer(i)}, device_id_type=MESH))
    each(n_arc - 1, lambda i: pl.semaphore_signal(barrier, inc=1, device_id={"arc": arc_peer(i)}, device_id_type=MESH))

    held = cols // PANEL
    for turn in range(2):
        chosen = [jnp.where(owner_ref[turn] == par * held + b, 1.0, 0.0) for b in range(held)]
        for half in range(PANEL // BLK):
            for band in range(rows // BLK):
                low, top = band * BLK, (band + 1) * BLK
                total = jnp.zeros((BLK, BLK), F32)
                for b in range(held):
                    block = b * (PANEL // BLK) + half
                    weight = mask_ref[band, block].astype(F32) * chosen[b]
                    total = total + obs_ref[low:top, block * BLK:(block + 1) * BLK] * weight
                at = turn * PANEL + half * BLK
                part_ref[low:top, at:at + BLK] = total

    pl.semaphore_wait(barrier, n_par + n_arc - 2)

    def part_copy(i):
        peer = par_peer(i)
        src = part_ref.at[pl.ds(pl.multiple_of(peer * share, 8), share)]
        return send(src, piece_ref.at[i], part_sems, i, {"par": peer})

    each(n_par - 1, lambda i: part_copy(i).start())
    each(n_par - 1, lambda i: part_copy(i).wait_recv())
    own_share = pl.ds(pl.multiple_of(par * share, 8), share)
    total = part_ref[own_share, :]
    for i in range(n_par - 1):
        total = total + piece_ref[i]
    panel_ref[own_share, :] = total

    def panel_copy(i):
        return send(panel_ref.at[own_share], panel_ref.at[own_share], panel_sems, i, {"par": par_peer(i)})

    each(n_par - 1, lambda i: panel_copy(i).start())
    each(n_par - 1, lambda i: panel_copy(i).wait_recv())

    panel = panel_ref[...]
    turned = panel.T
    for i in range(tiles):
        gram_rows = dot_nn(turned[i * TILE:(i + 1) * TILE], panel[:, :(i + 1) * TILE])
        for j in range(i + 1):
            at = (i * (i + 1) // 2 + j) * TILE
            gram_ref[at:at + TILE, :] = gram_rows[:, j * TILE:(j + 1) * TILE]

    def gram_copy(i):
        peer = arc_peer(i)
        at = pl.multiple_of((2 * par + peer % 2) * slice_rows, 8)
        return send(gram_ref.at[pl.ds(at, slice_rows)], gram_piece_ref.at[i], gram_sems, i, {"arc": peer})

    each(n_arc - 1, lambda i: gram_copy(i).start())

    high, low = halves(turned)
    stack_ref[...] = jnp.concatenate([high, high, low], 1)

    def owner_chip(t):
        side = t % 2
        across = chips - 1 - chip
        beside = chip + 1 - 2 * (chip % 2)
        return [
            (lax.rem(chip + 2, chips), lax.rem(chip + 2, chips)),
            (beside, across),
            (across, beside),
            (chip, chip),
        ][t // 2][side]

    def column_of(half, t):
        return pl.multiple_of((half * 8 + (t % 2) * 4 + owner_chip(t)) * width, BLK)

    def cross_tile(half, t):
        column = column_of(half, t)
        bands = []
        for band in range(rows // BLK):
            parts = [
                obs_ref[band * BLK:(band + 1) * BLK, pl.ds(pl.multiple_of(column + h * BLK, BLK), BLK)]
                * mask_ref[band, column // BLK + h].astype(F32)
                for h in range(width // BLK)
            ]
            bands.append(jnp.concatenate(parts, 1))
        up, down = halves(jnp.concatenate(bands, 0))
        return jnp.dot(stack_ref[...], jnp.concatenate([up, down, up], 0), preferred_element_type=F32)

    def core_copy(t):
        return send(to_core_ref.at[t], from_core_ref.at[t], core_sems, t, {"arc": arc + 1 - 2 * core})

    for t in range(8):
        to_core_ref[t] = cross_tile(1 - core, t)
        core_copy(t).start()

    each(n_arc - 1, lambda i: gram_copy(i).wait_recv())
    own_at = pl.multiple_of((2 * par + core) * slice_rows, 8)
    gram_total = gram_ref[pl.ds(own_at, slice_rows), :]
    for i in range(n_arc - 1):
        gram_total = gram_total + gram_piece_ref[i]
    gram_all_ref[par, core] = gram_total

    def all_copy(i):
        here = gram_all_ref.at[par, core]
        return send(here, here, all_sems, i, {"par": par_peer(i)})

    each(n_par - 1, lambda i: all_copy(i).start())

    def one_copy(t):
        to = (chip + 1 - 2 * (chip % 2)) if t % 2 == 0 else (chips - 1 - chip)
        return send(sums_ref.at[t], from_one_ref.at[t], one_sems, t, {"arc": 2 * to + core})

    for t in range(8):
        own = cross_tile(core, t)
        core_copy(t).wait_recv()
        sums_ref[t] = own + from_core_ref[t]
        if t < 4:
            one_copy(t).start()

    each(n_par - 1, lambda i: all_copy(i).wait_recv())
    fwd = send(gram_all_ref.at[:, core], gram_all_ref.at[:, core], fwd_sems, 0, {"arc": arc + 1 - 2 * core})
    fwd.start()
    fwd.wait_recv()
    flat = gram_all_ref[...].reshape(2 * n_par * slice_rows, TILE)
    for i in range(tiles):
        for j in range(i + 1):
            at = (i * (i + 1) // 2 + j) * TILE
            fac_ref[i * TILE:(i + 1) * TILE, j * TILE:(j + 1) * TILE] = flat[at:at + TILE]
        if i + 1 < tiles:
            fac_ref[i * TILE:(i + 1) * TILE, (i + 1) * TILE:] = jnp.zeros((TILE, order - (i + 1) * TILE), F32)

    def two_copy(t):
        to = (chips - 1 - chip) if t % 2 == 0 else (chip + 1 - 2 * (chip % 2))
        return send(sums_ref.at[4 + t], from_two_ref.at[t], two_sems, t, {"arc": 2 * to + core})

    for k in range(tiles):
        factor_step(fac_ref, k, tiles)
        if k == 1:
            for t in range(2):
                one_copy(t).wait_recv()
                sums_ref[4 + t] = sums_ref[4 + t] + from_one_ref[t]
                two_copy(t).start()

    def out_copy(t, i):
        peer = arc_peer(i)
        src = result_ref.at[t, pl.ds(pl.multiple_of(peer * out_rows, 8), out_rows)]
        dst = out_ref.at[:, pl.ds(column_of(core, 6 + t), width)]
        return send(src, dst, out_sems, t * (n_arc - 1) + i, {"arc": peer})

    for t in range(2):
        one_copy(2 + t).wait_recv()
        two_copy(t).wait_recv()
        whole = sums_ref[6 + t] + from_one_ref[2 + t] + from_two_ref[t]
        for i in range(tiles):
            depth = (i + 1) * TILE
            result_ref[t, i * TILE:depth] = dot_nn(fac_ref[i * TILE:depth, :depth], whole[:depth]) * scale
        each(n_arc - 1, lambda i: out_copy(t, i).start())
        out_ref[:, pl.ds(column_of(core, 6 + t), width)] = result_ref[
            t, pl.ds(pl.multiple_of(arc * out_rows, 8), out_rows)
        ]

    each(n_par - 1, lambda i: part_copy(i).wait_send())
    each(n_par - 1, lambda i: panel_copy(i).wait_send())
    each(n_arc - 1, lambda i: gram_copy(i).wait_send())
    each(n_par - 1, lambda i: all_copy(i).wait_send())
    fwd.wait_send()
    for t in range(8):
        core_copy(t).wait_send()
    for t in range(4):
        one_copy(t).wait_send()
    for t in range(2):
        two_copy(t).wait_send()
    for t in range(2):
        each(n_arc - 1, lambda i: out_copy(t, i).wait())


def shards(observations, arc_mask, panel_owner):
    n_arc, n_par = lax.axis_size("arc"), lax.axis_size("par")
    rows, cols = observations.shape
    order = 2 * PANEL
    share = rows // n_par
    width = cols // 16
    tiles = order // TILE
    slice_rows = tiles * (tiles + 1) // 2 * TILE // (2 * n_par)

    def pair(count):
        return pltpu.SemaphoreType.DMA((2, count))

    return pl.pallas_call(
        functools.partial(kernel, n_arc, n_par),
        out_shape=jax.ShapeDtypeStruct((order // n_arc, cols), F32),
        in_specs=[
            pl.BlockSpec(memory_space=pltpu.VMEM),
            pl.BlockSpec(memory_space=pltpu.SMEM),
            pl.BlockSpec(memory_space=pltpu.SMEM),
        ],
        out_specs=pl.BlockSpec(memory_space=pltpu.VMEM),
        scratch_shapes=[
            pltpu.VMEM((rows, order), F32),
            pltpu.VMEM((n_par - 1, share, order), F32),
            pltpu.VMEM((rows, order), F32),
            pltpu.VMEM((order, 3 * rows), BF16),
            pltpu.VMEM((2 * n_par * slice_rows, TILE), F32),
            pltpu.VMEM((n_arc - 1, slice_rows, TILE), F32),
            pltpu.VMEM((n_par, 2, slice_rows, TILE), F32),
            pltpu.VMEM((order, order), F32),
            pltpu.VMEM((8, order, width), F32),
            pltpu.VMEM((8, order, width), F32),
            pltpu.VMEM((8, order, width), F32),
            pltpu.VMEM((4, order, width), F32),
            pltpu.VMEM((2, order, width), F32),
            pltpu.VMEM((2, order, width), F32),
            pair(n_par - 1),
            pair(n_par - 1),
            pair(n_arc - 1),
            pair(n_par - 1),
            pair(1),
            pair(8),
            pair(4),
            pair(2),
            pair(2 * (n_arc - 1)),
        ],
        compiler_params=pltpu.CompilerParams(
            collective_id=0, has_side_effects=True, vmem_limit_bytes=48 << 20
        ),
        name="info_rows",
    )(observations, arc_mask, panel_owner)


def solution(mesh):
    return jax.shard_map(
        shards,
        mesh=mesh,
        in_specs=(P("arc", "par"), P("arc", "par"), P()),
        out_specs=P("arc", "par"),
        check_vma=False,
    )
```

time: 2390 us -> 88.6 us (0.04)
  local copies, waits for them, and re-layouts: 1070 us -> 4.49 us
  other arithmetic: 675 us -> 0 us
  waiting for transfers between devices: 316 us -> 0 us
  matrix products: 270 us -> 0 us
  Pallas kernels: 0 us -> 83.9 us
  loops' own time: 34.5 us -> 0 us
    select_n x1026 -> x0, other arithmetic: 337 us -> none  [the longest x512 333 us: one_column(): scaled = jnp.where(positions >= column, values / jnp.sqrt(pivot), 0.0)]
    div x513 -> x0, other arithmetic: 336 us -> none  [the longest x512 332 us: one_row(): new_row = (unit_row - matmul_high(lower_row, inverse)) / diag_entry]
    dynamic_update_slice x1024 -> x0, local copies, waits for them, and re-layouts: 336 us -> none  [the longest x512 314 us: one_column(): return lax.dynamic_update_slice_in_dim(lower, scaled, column, 1)]
    sqrt x512 -> x0, local copies, waits for them, and re-layouts: 332 us -> none  [one_column(): scaled = jnp.where(positions >= column, values / jnp.sqrt(pivot), 0.0)]
    dynamic_slice x512 -> x0, local copies, waits for them, and re-layouts: 321 us -> none  [one_row(): diag_entry = lax.dynamic_slice_in_dim(lower_row, index, 1, 1)]
    psum x4 -> x0, waiting for transfers between devices: 316 us -> none  [the longest x2 171 us: spread(): return lax.psum(jnp.where(mine, array, jnp.zeros_like(array)), axis)]
    dot_general x1032 -> x0, matrix products: 270 us -> none  [the longest x1028 251 us: matmul_high(): jnp.dot(left, right, precision=lax.Precision.HIGHEST, preferred_element_t...]
    pallas_call x0 -> x1, Pallas kernels: none -> 83.9 us  [shards(): pl.pallas_call(functools.partial(kernel, n_arc, n_par), out_shape=jax.Sha...]
where the time goes in v2:
time: 88.6 us; the launch traced here: 88.4 us
  Pallas kernels  83.9 us (95%)
  local copies, waits for them, and re-layouts  4.49 us (5%)
    pallas_call x1, Pallas kernels, shards(): pl.pallas_call(functools.partial(kernel, n_arc, n_par), out_shape=jax.Sha...  83.9 us
    unnamed x7, local copies, waits for them, and re-layouts  4.49 us

profile of v2, /device:TPU:1, one launch (start us, length us, event | category | flops | bytes accessed | tf_op | source)
XLA Modules:
  0.0 88.4 jit_solution(13527146010855137837)
XLA Ops:
  0.0 0.0 copy-start
  0.0 2.2 %copy-done = f32[256,4096]{1,0:T(8,128)S(1)} copy-done((f32[256,4096]{1,0:T(8,128)S(1)}, f32[256,4096]{1,0:T(8,128)}, u32[]{:S(2)}) %copy-start) | copy-done | bytes 4194328
  2.2 0.0 copy-start.1
  2.2 0.7 copy-done.1
  2.9 0.0 copy-start.2
  2.9 0.7 copy-done.2
  3.5 83.9 %info_rows.1 = f32[64,4096]{1,0:T(8,128)S(1)} custom-call(f32[256,4096]{1,0:T(8,128)S(1)} %copy-done, s32[2,32]{1,0:T(2,128)S(1)} %copy-done.1, s32[2]{0:T(128)S(1)} %copy-done.2), custom_call_target="tpu_custom_call" | custom-call | tf_op jit(solution)/shard_map/info_rows/pallas_call | solution.py:306
  87.4 1.0 %copy.5 = f32[64,4096]{1,0:T(8,128)} copy(f32[64,4096]{1,0:T(8,128)S(1)} %info_rows.1) | data formatting | bytes 2097152
Async XLA Ops:
  0.0 2.2 %copy-start = (f32[256,4096]{1,0:T(8,128)S(1)}, f32[256,4096]{1,0:T(8,128)}, u32[]{:S(2)}) copy-start(f32[256,4096]{1,0:T(8,128)} %obs_ref.1) | copy-start | bytes 12582916
  2.2 0.7 copy-start.1
  2.9 0.7 copy-start.2

commit v3 on v2

--- a/solution.py
+++ b/solution.py
@@ -84,11 +84,12 @@
 
 def kernel(
     n_arc, n_par,
-    obs_ref, mask_ref, owner_ref, out_ref,
-    part_ref, piece_ref, panel_ref, stack_ref,
+    obs_hbm, mask_hbm, owner_hbm, out_ref,
+    obs_ref, mask_ref, owner_ref,
+    part_ref, piece_ref, panel_ref, other_obs_ref, other_panel_ref, stack_ref,
     gram_ref, gram_piece_ref, gram_all_ref, fac_ref,
-    to_core_ref, from_core_ref, sums_ref, from_one_ref, from_two_ref, result_ref,
-    part_sems, panel_sems, gram_sems, all_sems, fwd_sems, core_sems, one_sems, two_sems, out_sems,
+    sums_ref, from_one_ref, from_two_ref, result_ref,
+    load_sems, part_sems, last_sems, panel_sems, gram_sems, all_sems, core_sems, one_sems, two_sems, out_sems,
 ):
     rows, cols = obs_ref.shape
     order = 2 * PANEL
@@ -119,46 +120,95 @@
     def arc_peer(i):
         return lax.rem(arc + i + 1, n_arc)
 
+    sibling = {"arc": arc + 1 - 2 * core}
+    loads = [
+        pltpu.make_async_copy(src, dst, load_sems.at[i])
+        for i, (src, dst) in enumerate([(mask_hbm, mask_ref), (owner_hbm, owner_ref), (obs_hbm, obs_ref)])
+    ]
+    for load in loads:
+        load.start()
+
     barrier = pltpu.get_barrier_semaphore()
     each(n_par - 1, lambda i: pl.semaphore_signal(barrier, inc=1, device_id={"par": par_peer(i)}, device_id_type=MESH))
     each(n_arc - 1, lambda i: pl.semaphore_signal(barrier, inc=1, device_id={"arc": arc_peer(i)}, device_id_type=MESH))
+    for load in loads:
+        load.wait()
 
     held = cols // PANEL
-    for turn in range(2):
-        chosen = [jnp.where(owner_ref[turn] == par * held + b, 1.0, 0.0) for b in range(held)]
-        for half in range(PANEL // BLK):
-            for band in range(rows // BLK):
-                low, top = band * BLK, (band + 1) * BLK
-                total = jnp.zeros((BLK, BLK), F32)
-                for b in range(held):
-                    block = b * (PANEL // BLK) + half
-                    weight = mask_ref[band, block].astype(F32) * chosen[b]
-                    total = total + obs_ref[low:top, block * BLK:(block + 1) * BLK] * weight
-                at = turn * PANEL + half * BLK
-                part_ref[low:top, at:at + BLK] = total
+    last = n_par * held - 1
+    last_first = owner_ref[0] == last
+    other = jnp.where(last_first, owner_ref[1], owner_ref[0])
+    chosen = [jnp.where(other == par * held + b, 1.0, 0.0) for b in range(held)]
+    for half in range(PANEL // BLK):
+        for band in range(rows // BLK):
+            low, top = band * BLK, (band + 1) * BLK
+            total = jnp.zeros((BLK, BLK), F32)
+            for b in range(held):
+                block = b * (PANEL // BLK) + half
+                left, right = block * BLK, (block + 1) * BLK
+                masked = obs_ref[low:top, left:right] * mask_ref[band, block].astype(F32)
+                obs_ref[low:top, left:right] = masked
+                total = total + masked * chosen[b]
+            part_ref[low:top, half * BLK:(half + 1) * BLK] = total
 
     pl.semaphore_wait(barrier, n_par + n_arc - 2)
+
+    def share_of(device):
+        return pl.ds(pl.multiple_of(device * share, 8), share)
 
     def part_copy(i):
         peer = par_peer(i)
-        src = part_ref.at[pl.ds(pl.multiple_of(peer * share, 8), share)]
-        return send(src, piece_ref.at[i], part_sems, i, {"par": peer})
+        return send(part_ref.at[share_of(peer)], piece_ref.at[i], part_sems, i, {"par": peer})
+
+    def last_copy(i):
+        peer = par_peer(i)
+        return send(
+            obs_ref.at[share_of(peer), cols - PANEL:], panel_ref.at[share_of(peer), PANEL:], last_sems, peer, {"par": peer}
+        )
+
+    def last_arrival():
+        here = panel_ref.at[share_of(par), PANEL:]
+        return send(here, here, last_sems, par, {"par": n_par - 1})
+
+    def obs_copy():
+        there = pl.ds(pl.multiple_of((1 - core) * (cols // 2), BLK), cols // 2)
+        return send(obs_ref.at[:, there], other_obs_ref, core_sems, 0, sibling)
+
+    def sibling_panel_copy():
+        return send(panel_ref, other_panel_ref, core_sems, 1, sibling)
+
+    owns_last = par == n_par - 1
+    own_share = share_of(par)
+
+    @pl.when(owns_last)
+    def _():
+        each(n_par - 1, lambda i: last_copy(i).start())
+        panel_ref[own_share, PANEL:] = obs_ref[own_share, cols - PANEL:]
 
     each(n_par - 1, lambda i: part_copy(i).start())
+    obs_copy().start()
     each(n_par - 1, lambda i: part_copy(i).wait_recv())
-    own_share = pl.ds(pl.multiple_of(par * share, 8), share)
     total = part_ref[own_share, :]
     for i in range(n_par - 1):
         total = total + piece_ref[i]
-    panel_ref[own_share, :] = total
+    panel_ref[own_share, :PANEL] = total
+
+    @pl.when(jnp.logical_not(owns_last))
+    def _():
+        last_arrival().wait_recv()
 
     def panel_copy(i):
         return send(panel_ref.at[own_share], panel_ref.at[own_share], panel_sems, i, {"par": par_peer(i)})
 
     each(n_par - 1, lambda i: panel_copy(i).start())
     each(n_par - 1, lambda i: panel_copy(i).wait_recv())
-
-    panel = panel_ref[...]
+    sibling_panel_copy().start()
+
+    def in_order(ref):
+        one, two = ref[:, :PANEL], ref[:, PANEL:]
+        return jnp.concatenate([jnp.where(last_first, two, one), jnp.where(last_first, one, two)], 1)
+
+    panel = in_order(panel_ref)
     turned = panel.T
     for i in range(tiles):
         gram_rows = dot_nn(turned[i * TILE:(i + 1) * TILE], panel[:, :(i + 1) * TILE])
@@ -173,8 +223,13 @@
 
     each(n_arc - 1, lambda i: gram_copy(i).start())
 
-    high, low = halves(turned)
-    stack_ref[...] = jnp.concatenate([high, high, low], 1)
+    def fill_stack(at, turned_panel):
+        high, low = halves(turned_panel)
+        stack_ref[:, at:at + 3 * rows] = jnp.concatenate([high, high, low], 1)
+
+    fill_stack(0, turned)
+    sibling_panel_copy().wait_recv()
+    fill_stack(3 * rows, in_order(other_panel_ref).T)
 
     def owner_chip(t):
         side = t % 2
@@ -187,28 +242,25 @@
             (chip, chip),
         ][t // 2][side]
 
-    def column_of(half, t):
-        return pl.multiple_of((half * 8 + (t % 2) * 4 + owner_chip(t)) * width, BLK)
-
-    def cross_tile(half, t):
-        column = column_of(half, t)
-        bands = []
-        for band in range(rows // BLK):
-            parts = [
-                obs_ref[band * BLK:(band + 1) * BLK, pl.ds(pl.multiple_of(column + h * BLK, BLK), BLK)]
-                * mask_ref[band, column // BLK + h].astype(F32)
-                for h in range(width // BLK)
-            ]
-            bands.append(jnp.concatenate(parts, 1))
-        up, down = halves(jnp.concatenate(bands, 0))
-        return jnp.dot(stack_ref[...], jnp.concatenate([up, down, up], 0), preferred_element_type=F32)
-
-    def core_copy(t):
-        return send(to_core_ref.at[t], from_core_ref.at[t], core_sems, t, {"arc": arc + 1 - 2 * core})
-
-    for t in range(8):
-        to_core_ref[t] = cross_tile(1 - core, t)
-        core_copy(t).start()
+    def column_of(t):
+        return pl.multiple_of(((t % 2) * 4 + owner_chip(t)) * width, BLK)
+
+    def cross_tile(t):
+        own = obs_ref[:, pl.ds(pl.multiple_of(core * (cols // 2) + column_of(t), BLK), width)]
+        theirs = other_obs_ref[:, pl.ds(column_of(t), width)]
+        up, down = halves(own)
+        their_up, their_down = halves(theirs)
+        stacked = jnp.concatenate([up, down, up, their_up, their_down, their_up], 0)
+        return jnp.dot(stack_ref[...], stacked, preferred_element_type=F32)
+
+    def one_copy(t):
+        to = (chip + 1 - 2 * (chip % 2)) if t % 2 == 0 else (chips - 1 - chip)
+        return send(sums_ref.at[t], from_one_ref.at[t], one_sems, t, {"arc": 2 * to + core})
+
+    obs_copy().wait_recv()
+    for t in range(4):
+        sums_ref[t] = cross_tile(t)
+        one_copy(t).start()
 
     each(n_arc - 1, lambda i: gram_copy(i).wait_recv())
     own_at = pl.multiple_of((2 * par + core) * slice_rows, 8)
@@ -223,19 +275,11 @@
 
     each(n_par - 1, lambda i: all_copy(i).start())
 
-    def one_copy(t):
-        to = (chip + 1 - 2 * (chip % 2)) if t % 2 == 0 else (chips - 1 - chip)
-        return send(sums_ref.at[t], from_one_ref.at[t], one_sems, t, {"arc": 2 * to + core})
-
-    for t in range(8):
-        own = cross_tile(core, t)
-        core_copy(t).wait_recv()
-        sums_ref[t] = own + from_core_ref[t]
-        if t < 4:
-            one_copy(t).start()
+    for t in range(4, 8):
+        sums_ref[t] = cross_tile(t)
 
     each(n_par - 1, lambda i: all_copy(i).wait_recv())
-    fwd = send(gram_all_ref.at[:, core], gram_all_ref.at[:, core], fwd_sems, 0, {"arc": arc + 1 - 2 * core})
+    fwd = send(gram_all_ref.at[:, core], gram_all_ref.at[:, core], core_sems, 2, sibling)
     fwd.start()
     fwd.wait_recv()
     flat = gram_all_ref[...].reshape(2 * n_par * slice_rows, TILE)
@@ -258,10 +302,13 @@
                 sums_ref[4 + t] = sums_ref[4 + t] + from_one_ref[t]
                 two_copy(t).start()
 
+    def out_column(t):
+        return pl.multiple_of(core * (cols // 2) + column_of(6 + t), BLK)
+
     def out_copy(t, i):
         peer = arc_peer(i)
         src = result_ref.at[t, pl.ds(pl.multiple_of(peer * out_rows, 8), out_rows)]
-        dst = out_ref.at[:, pl.ds(column_of(core, 6 + t), width)]
+        dst = out_ref.at[:, pl.ds(out_column(t), width)]
         return send(src, dst, out_sems, t * (n_arc - 1) + i, {"arc": peer})
 
     for t in range(2):
@@ -272,7 +319,7 @@
             depth = (i + 1) * TILE
             result_ref[t, i * TILE:depth] = dot_nn(fac_ref[i * TILE:depth, :depth], whole[:depth]) * scale
         each(n_arc - 1, lambda i: out_copy(t, i).start())
-        out_ref[:, pl.ds(column_of(core, 6 + t), width)] = result_ref[
+        out_ref[:, pl.ds(out_column(t), width)] = result_ref[
             t, pl.ds(pl.multiple_of(arc * out_rows, 8), out_rows)
         ]
 
@@ -281,8 +328,13 @@
     each(n_arc - 1, lambda i: gram_copy(i).wait_send())
     each(n_par - 1, lambda i: all_copy(i).wait_send())
     fwd.wait_send()
-    for t in range(8):
-        core_copy(t).wait_send()
+    obs_copy().wait_send()
+    sibling_panel_copy().wait_send()
+
+    @pl.when(owns_last)
+    def _():
+        each(n_par - 1, lambda i: last_copy(i).wait_send())
+
     for t in range(4):
         one_copy(t).wait_send()
     for t in range(2):
@@ -306,39 +358,39 @@
     return pl.pallas_call(
         functools.partial(kernel, n_arc, n_par),
         out_shape=jax.ShapeDtypeStruct((order // n_arc, cols), F32),
-        in_specs=[
-            pl.BlockSpec(memory_space=pltpu.VMEM),
-            pl.BlockSpec(memory_space=pltpu.SMEM),
-            pl.BlockSpec(memory_space=pltpu.SMEM),
-        ],
+        in_specs=[pl.BlockSpec(memory_space=pl.ANY)] * 3,
         out_specs=pl.BlockSpec(memory_space=pltpu.VMEM),
         scratch_shapes=[
+            pltpu.VMEM((rows, cols), F32),
+            pltpu.SMEM(arc_mask.shape, jnp.int32),
+            pltpu.SMEM(panel_owner.shape, jnp.int32),
+            pltpu.VMEM((rows, PANEL), F32),
+            pltpu.VMEM((n_par - 1, share, PANEL), F32),
             pltpu.VMEM((rows, order), F32),
-            pltpu.VMEM((n_par - 1, share, order), F32),
+            pltpu.VMEM((rows, cols // 2), F32),
             pltpu.VMEM((rows, order), F32),
-            pltpu.VMEM((order, 3 * rows), BF16),
+            pltpu.VMEM((order, 6 * rows), BF16),
             pltpu.VMEM((2 * n_par * slice_rows, TILE), F32),
             pltpu.VMEM((n_arc - 1, slice_rows, TILE), F32),
             pltpu.VMEM((n_par, 2, slice_rows, TILE), F32),
             pltpu.VMEM((order, order), F32),
             pltpu.VMEM((8, order, width), F32),
-            pltpu.VMEM((8, order, width), F32),
-            pltpu.VMEM((8, order, width), F32),
             pltpu.VMEM((4, order, width), F32),
             pltpu.VMEM((2, order, width), F32),
             pltpu.VMEM((2, order, width), F32),
+            pltpu.SemaphoreType.DMA((3,)),
             pair(n_par - 1),
+            pair(n_par),
             pair(n_par - 1),
             pair(n_arc - 1),
             pair(n_par - 1),
-            pair(1),
-            pair(8),
+            pair(3),
             pair(4),
             pair(2),
             pair(2 * (n_arc - 1)),
         ],
         compiler_params=pltpu.CompilerParams(
-            collective_id=0, has_side_effects=True, vmem_limit_bytes=48 << 20
+            collective_id=0, has_side_effects=True, vmem_limit_bytes=60 << 20
         ),
         name="info_rows",
     )(observations, arc_mask, panel_owner)

time: 88.6 us -> 83.5 us (0.942)
  Pallas kernels: 83.9 us -> 81.1 us
  local copies, waits for them, and re-layouts: 4.49 us -> 2.27 us
    pallas_call x1, Pallas kernels: 83.9 us -> 81.1 us  [shards(): pl.pallas_call(functools.partial(kernel, n_arc, n_par), out_shape=jax.Sha...]
    unnamed x7 -> x1, local copies, waits for them, and re-layouts: 4.49 us -> 2.27 us
where the time goes in v3:
time: 83.5 us; the launch traced here: 83.3 us
  Pallas kernels  81.1 us (97%)
  local copies, waits for them, and re-layouts  2.27 us (3%)
    pallas_call x1, Pallas kernels, shards(): pl.pallas_call(functools.partial(kernel, n_arc, n_par), out_shape=jax.Sha...  81.1 us
    unnamed x1, local copies, waits for them, and re-layouts  2.27 us

profile of v3, /device:TPU:1, one launch (start us, length us, event | category | flops | bytes accessed | tf_op | source)
XLA Modules:
  0.0 83.3 jit_solution(5264826772392303383)
XLA Ops:
  0.0 81.1 %info_rows.1 = f32[64,4096]{1,0:T(8,128)} custom-call(f32[256,4096]{1,0:T(8,128)} %obs_hbm.1, s32[2,32]{1,0:T(2,128)} %mask_hbm.1, s32[2]{0:T(128)} %owner_hbm.1), custom_call_target="tpu_custom_call" | custom-call | tf_op jit(solution)/shard_map/info_rows/pallas_call | solution.py:358
  81.1 2.3 %copy.5 = f32[64,4096]{1,0:T(8,128)} copy(f32[64,4096]{1,0:T(8,128)} %info_rows.1) | data formatting | bytes 2097152

commit v4 on v3

--- a/solution.py
+++ b/solution.py
@@ -89,7 +89,7 @@
     part_ref, piece_ref, panel_ref, other_obs_ref, other_panel_ref, stack_ref,
     gram_ref, gram_piece_ref, gram_all_ref, fac_ref,
     sums_ref, from_one_ref, from_two_ref, result_ref,
-    load_sems, part_sems, last_sems, panel_sems, gram_sems, all_sems, core_sems, one_sems, two_sems, out_sems,
+    load_sems, part_sems, panel_sems, gram_sems, all_sems, core_sems, one_sems, two_sems, out_sems,
 ):
     rows, cols = obs_ref.shape
     order = 2 * PANEL
@@ -158,17 +158,15 @@
 
     def part_copy(i):
         peer = par_peer(i)
-        return send(part_ref.at[share_of(peer)], piece_ref.at[i], part_sems, i, {"par": peer})
-
-    def last_copy(i):
+        return send(part_ref.at[share_of(peer), :PANEL], piece_ref.at[i, :, :PANEL], part_sems, 0, {"par": peer})
+
+    def both_copy(i):
         peer = par_peer(i)
-        return send(
-            obs_ref.at[share_of(peer), cols - PANEL:], panel_ref.at[share_of(peer), PANEL:], last_sems, peer, {"par": peer}
-        )
-
-    def last_arrival():
-        here = panel_ref.at[share_of(par), PANEL:]
-        return send(here, here, last_sems, par, {"par": n_par - 1})
+        return send(part_ref.at[share_of(peer)], piece_ref.at[i], part_sems, 1, {"par": peer})
+
+    def parts(count):
+        some = piece_ref.at[:count, :, :PANEL]
+        return send(some, some, part_sems, 0, {"par": par_peer(0)})
 
     def obs_copy():
         there = pl.ds(pl.multiple_of((1 - core) * (cols // 2), BLK), cols // 2)
@@ -182,26 +180,40 @@
 
     @pl.when(owns_last)
     def _():
-        each(n_par - 1, lambda i: last_copy(i).start())
-        panel_ref[own_share, PANEL:] = obs_ref[own_share, cols - PANEL:]
-
-    each(n_par - 1, lambda i: part_copy(i).start())
+        part_ref[:, PANEL:] = obs_ref[:, cols - PANEL:]
+        each(n_par - 1, lambda i: both_copy(i).start())
+
+    @pl.when(jnp.logical_not(owns_last))
+    def _():
+        each(n_par - 1, lambda i: part_copy(i).start())
+
     obs_copy().start()
-    each(n_par - 1, lambda i: part_copy(i).wait_recv())
-    total = part_ref[own_share, :]
+
+    @pl.when(owns_last)
+    def _():
+        parts(n_par - 1).wait_recv()
+        panel_ref[own_share, PANEL:] = part_ref[own_share, PANEL:]
+
+    @pl.when(jnp.logical_not(owns_last))
+    def _():
+        parts(n_par - 2).wait_recv()
+        both_copy(par).wait_recv()
+        panel_ref[own_share, PANEL:] = piece_ref[par, :, PANEL:]
+
+    total = part_ref[own_share, :PANEL]
     for i in range(n_par - 1):
-        total = total + piece_ref[i]
+        total = total + piece_ref[i, :, :PANEL]
     panel_ref[own_share, :PANEL] = total
 
-    @pl.when(jnp.logical_not(owns_last))
-    def _():
-        last_arrival().wait_recv()
-
     def panel_copy(i):
-        return send(panel_ref.at[own_share], panel_ref.at[own_share], panel_sems, i, {"par": par_peer(i)})
+        return send(panel_ref.at[own_share], panel_ref.at[own_share], panel_sems, 0, {"par": par_peer(i)})
+
+    def panel_all():
+        others = panel_ref.at[:share * (n_par - 1)]
+        return send(others, others, panel_sems, 0, {"par": par_peer(0)})
 
     each(n_par - 1, lambda i: panel_copy(i).start())
-    each(n_par - 1, lambda i: panel_copy(i).wait_recv())
+    panel_all().wait_recv()
     sibling_panel_copy().start()
 
     def in_order(ref):
@@ -271,14 +283,18 @@
 
     def all_copy(i):
         here = gram_all_ref.at[par, core]
-        return send(here, here, all_sems, i, {"par": par_peer(i)})
+        return send(here, here, all_sems, 0, {"par": par_peer(i)})
+
+    def all_all():
+        others = gram_all_ref.at[:n_par - 1, core]
+        return send(others, others, all_sems, 0, {"par": par_peer(0)})
 
     each(n_par - 1, lambda i: all_copy(i).start())
 
     for t in range(4, 8):
         sums_ref[t] = cross_tile(t)
 
-    each(n_par - 1, lambda i: all_copy(i).wait_recv())
+    all_all().wait_recv()
     fwd = send(gram_all_ref.at[:, core], gram_all_ref.at[:, core], core_sems, 2, sibling)
     fwd.start()
     fwd.wait_recv()
@@ -290,9 +306,14 @@
         if i + 1 < tiles:
             fac_ref[i * TILE:(i + 1) * TILE, (i + 1) * TILE:] = jnp.zeros((TILE, order - (i + 1) * TILE), F32)
 
-    def two_copy(t):
+    part = width // 2
+
+    def two_copy(t, h):
         to = (chips - 1 - chip) if t % 2 == 0 else (chip + 1 - 2 * (chip % 2))
-        return send(sums_ref.at[4 + t], from_two_ref.at[t], two_sems, t, {"arc": 2 * to + core})
+        columns = pl.ds(h * part, part)
+        return send(
+            sums_ref.at[4 + t, :, columns], from_two_ref.at[t, :, columns], two_sems, 2 * t + h, {"arc": 2 * to + core}
+        )
 
     for k in range(tiles):
         factor_step(fac_ref, k, tiles)
@@ -300,47 +321,55 @@
             for t in range(2):
                 one_copy(t).wait_recv()
                 sums_ref[4 + t] = sums_ref[4 + t] + from_one_ref[t]
-                two_copy(t).start()
-
-    def out_column(t):
-        return pl.multiple_of(core * (cols // 2) + column_of(6 + t), BLK)
-
-    def out_copy(t, i):
+                two_copy(t, 0).start()
+            for t in range(2):
+                two_copy(t, 1).start()
+
+    def out_column(t, h):
+        return pl.multiple_of(core * (cols // 2) + column_of(6 + t) + h * part, BLK)
+
+    def out_copy(t, h, i):
         peer = arc_peer(i)
-        src = result_ref.at[t, pl.ds(pl.multiple_of(peer * out_rows, 8), out_rows)]
-        dst = out_ref.at[:, pl.ds(out_column(t), width)]
-        return send(src, dst, out_sems, t * (n_arc - 1) + i, {"arc": peer})
-
-    for t in range(2):
-        one_copy(2 + t).wait_recv()
-        two_copy(t).wait_recv()
-        whole = sums_ref[6 + t] + from_one_ref[2 + t] + from_two_ref[t]
-        for i in range(tiles):
-            depth = (i + 1) * TILE
-            result_ref[t, i * TILE:depth] = dot_nn(fac_ref[i * TILE:depth, :depth], whole[:depth]) * scale
-        each(n_arc - 1, lambda i: out_copy(t, i).start())
-        out_ref[:, pl.ds(out_column(t), width)] = result_ref[
-            t, pl.ds(pl.multiple_of(arc * out_rows, 8), out_rows)
-        ]
-
-    each(n_par - 1, lambda i: part_copy(i).wait_send())
-    each(n_par - 1, lambda i: panel_copy(i).wait_send())
+        src = result_ref.at[t, pl.ds(pl.multiple_of(peer * out_rows, 8), out_rows), h * part:(h + 1) * part]
+        dst = out_ref.at[:, pl.ds(out_column(t, h), part)]
+        return send(src, dst, out_sems, (2 * t + h) * (n_arc - 1) + i, {"arc": peer})
+
+    for h in range(2):
+        for t in range(2):
+            left, right = h * part, (h + 1) * part
+            if h == 0:
+                one_copy(2 + t).wait_recv()
+            two_copy(t, h).wait_recv()
+            whole = sums_ref[6 + t, :, left:right] + from_one_ref[2 + t, :, left:right] + from_two_ref[t, :, left:right]
+            for i in range(tiles):
+                depth = (i + 1) * TILE
+                result_ref[t, i * TILE:depth, left:right] = dot_nn(fac_ref[i * TILE:depth, :depth], whole[:depth]) * scale
+            each(n_arc - 1, lambda i: out_copy(t, h, i).start())
+            out_ref[:, pl.ds(out_column(t, h), part)] = result_ref[
+                t, pl.ds(pl.multiple_of(arc * out_rows, 8), out_rows), left:right
+            ]
+
+    @pl.when(owns_last)
+    def _():
+        send(piece_ref, piece_ref, part_sems, 1, {"par": par_peer(0)}).wait_send()
+
+    @pl.when(jnp.logical_not(owns_last))
+    def _():
+        parts(n_par - 1).wait_send()
+
+    panel_all().wait_send()
     each(n_arc - 1, lambda i: gram_copy(i).wait_send())
-    each(n_par - 1, lambda i: all_copy(i).wait_send())
+    all_all().wait_send()
     fwd.wait_send()
     obs_copy().wait_send()
     sibling_panel_copy().wait_send()
 
-    @pl.when(owns_last)
-    def _():
-        each(n_par - 1, lambda i: last_copy(i).wait_send())
-
     for t in range(4):
         one_copy(t).wait_send()
     for t in range(2):
-        two_copy(t).wait_send()
-    for t in range(2):
-        each(n_arc - 1, lambda i: out_copy(t, i).wait())
+        for h in range(2):
+            two_copy(t, h).wait_send()
+            each(n_arc - 1, lambda i: out_copy(t, h, i).wait())
 
 
 def shards(observations, arc_mask, panel_owner):
@@ -364,8 +393,8 @@
             pltpu.VMEM((rows, cols), F32),
             pltpu.SMEM(arc_mask.shape, jnp.int32),
             pltpu.SMEM(panel_owner.shape, jnp.int32),
-            pltpu.VMEM((rows, PANEL), F32),
-            pltpu.VMEM((n_par - 1, share, PANEL), F32),
+            pltpu.VMEM((rows, order), F32),
+            pltpu.VMEM((n_par - 1, share, order), F32),
             pltpu.VMEM((rows, order), F32),
             pltpu.VMEM((rows, cols // 2), F32),
             pltpu.VMEM((rows, order), F32),
@@ -379,15 +408,14 @@
             pltpu.VMEM((2, order, width), F32),
             pltpu.VMEM((2, order, width), F32),
             pltpu.SemaphoreType.DMA((3,)),
-            pair(n_par - 1),
-            pair(n_par),
-            pair(n_par - 1),
+            pair(2),
+            pair(1),
             pair(n_arc - 1),
-            pair(n_par - 1),
+            pair(1),
             pair(3),
             pair(4),
-            pair(2),
-            pair(2 * (n_arc - 1)),
+            pair(4),
+            pair(4 * (n_arc - 1)),
         ],
         compiler_params=pltpu.CompilerParams(
             collective_id=0, has_side_effects=True, vmem_limit_bytes=60 << 20

time: 83.5 us -> 79.5 us (0.952)
  Pallas kernels: 81.1 us -> 77.1 us
    pallas_call x1, Pallas kernels: 81.1 us -> 77.1 us  [shards(): pl.pallas_call(functools.partial(kernel, n_arc, n_par), out_shape=jax.Sha...]
where the time goes in v4:
time: 79.5 us; the launch traced here: 79.3 us
  Pallas kernels  77.1 us (97%)
  local copies, waits for them, and re-layouts  2.27 us (3%)
    pallas_call x1, Pallas kernels, shards(): pl.pallas_call(functools.partial(kernel, n_arc, n_par), out_shape=jax.Sha...  77.1 us
    unnamed x1, local copies, waits for them, and re-layouts  2.27 us

profile of v4, /device:TPU:1, one launch (start us, length us, event | category | flops | bytes accessed | tf_op | source)
XLA Modules:
  0.0 79.3 jit_solution(17352765536431678514)
XLA Ops:
  0.0 77.1 %info_rows.1 = f32[64,4096]{1,0:T(8,128)} custom-call(f32[256,4096]{1,0:T(8,128)} %obs_hbm.1, s32[2,32]{1,0:T(2,128)} %mask_hbm.1, s32[2]{0:T(128)} %owner_hbm.1), custom_call_target="tpu_custom_call" | custom-call | tf_op jit(solution)/shard_map/info_rows/pallas_call | solution.py:387
  77.1 2.3 %copy.5 = f32[64,4096]{1,0:T(8,128)} copy(f32[64,4096]{1,0:T(8,128)} %info_rows.1) | data formatting | bytes 2097152

commit v5 on v4

--- a/solution.py
+++ b/solution.py
@@ -86,7 +86,7 @@
     n_arc, n_par,
     obs_hbm, mask_hbm, owner_hbm, out_ref,
     obs_ref, mask_ref, owner_ref,
-    part_ref, piece_ref, panel_ref, other_obs_ref, other_panel_ref, stack_ref,
+    part_ref, piece_ref, panel_ref, other_obs_ref, other_panel_ref, turned_ref, stack_ref,
     gram_ref, gram_piece_ref, gram_all_ref, fac_ref,
     sums_ref, from_one_ref, from_two_ref, result_ref,
     load_sems, part_sems, panel_sems, gram_sems, all_sems, core_sems, one_sems, two_sems, out_sems,
@@ -115,7 +115,7 @@
         lax.fori_loop(0, count, lambda i, carry: (body(i), carry)[1], 0)
 
     def par_peer(i):
-        return lax.rem(par + i + 1, n_par)
+        return lax.rem(par + lax.rem(i * 4, n_par - 1) + 1, n_par)
 
     def arc_peer(i):
         return lax.rem(arc + i + 1, n_arc)
@@ -197,8 +197,9 @@
     @pl.when(jnp.logical_not(owns_last))
     def _():
         parts(n_par - 2).wait_recv()
-        both_copy(par).wait_recv()
-        panel_ref[own_share, PANEL:] = piece_ref[par, :, PANEL:]
+        slot = lax.rem(par * 4, n_par - 1)
+        both_copy(slot).wait_recv()
+        panel_ref[own_share, PANEL:] = piece_ref[slot, :, PANEL:]
 
     total = part_ref[own_share, :PANEL]
     for i in range(n_par - 1):
@@ -222,15 +223,18 @@
 
     panel = in_order(panel_ref)
     turned = panel.T
+    turned_ref[...] = turned
+    band_rows = TILE // n_par
+    picked = [turned_ref[pl.ds(pl.multiple_of(i * TILE + par * band_rows, 8), band_rows), :] for i in range(tiles)]
+    gram_rows = dot_nn(jnp.concatenate(picked, 0), panel)
     for i in range(tiles):
-        gram_rows = dot_nn(turned[i * TILE:(i + 1) * TILE], panel[:, :(i + 1) * TILE])
         for j in range(i + 1):
-            at = (i * (i + 1) // 2 + j) * TILE
-            gram_ref[at:at + TILE, :] = gram_rows[:, j * TILE:(j + 1) * TILE]
+            at = (i * (i + 1) // 2 + j) * band_rows
+            gram_ref[at:at + band_rows, :] = gram_rows[i * band_rows:(i + 1) * band_rows, j * TILE:(j + 1) * TILE]
 
     def gram_copy(i):
         peer = arc_peer(i)
-        at = pl.multiple_of((2 * par + peer % 2) * slice_rows, 8)
+        at = pl.multiple_of(peer % 2 * slice_rows, 8)
         return send(gram_ref.at[pl.ds(at, slice_rows)], gram_piece_ref.at[i], gram_sems, i, {"arc": peer})
 
     each(n_arc - 1, lambda i: gram_copy(i).start())
@@ -275,7 +279,7 @@
         one_copy(t).start()
 
     each(n_arc - 1, lambda i: gram_copy(i).wait_recv())
-    own_at = pl.multiple_of((2 * par + core) * slice_rows, 8)
+    own_at = pl.multiple_of(core * slice_rows, 8)
     gram_total = gram_ref[pl.ds(own_at, slice_rows), :]
     for i in range(n_arc - 1):
         gram_total = gram_total + gram_piece_ref[i]
@@ -298,11 +302,11 @@
     fwd = send(gram_all_ref.at[:, core], gram_all_ref.at[:, core], core_sems, 2, sibling)
     fwd.start()
     fwd.wait_recv()
-    flat = gram_all_ref[...].reshape(2 * n_par * slice_rows, TILE)
     for i in range(tiles):
         for j in range(i + 1):
-            at = (i * (i + 1) // 2 + j) * TILE
-            fac_ref[i * TILE:(i + 1) * TILE, j * TILE:(j + 1) * TILE] = flat[at:at + TILE]
+            half, at = divmod((i * (i + 1) // 2 + j) * band_rows, slice_rows)
+            block = gram_all_ref[:, half, at:at + band_rows, :].reshape(TILE, TILE)
+            fac_ref[i * TILE:(i + 1) * TILE, j * TILE:(j + 1) * TILE] = block
         if i + 1 < tiles:
             fac_ref[i * TILE:(i + 1) * TILE, (i + 1) * TILE:] = jnp.zeros((TILE, order - (i + 1) * TILE), F32)
 
@@ -398,8 +402,9 @@
             pltpu.VMEM((rows, order), F32),
             pltpu.VMEM((rows, cols // 2), F32),
             pltpu.VMEM((rows, order), F32),
+            pltpu.VMEM((order, rows), F32),
             pltpu.VMEM((order, 6 * rows), BF16),
-            pltpu.VMEM((2 * n_par * slice_rows, TILE), F32),
+            pltpu.VMEM((2 * slice_rows, TILE), F32),
             pltpu.VMEM((n_arc - 1, slice_rows, TILE), F32),
             pltpu.VMEM((n_par, 2, slice_rows, TILE), F32),
             pltpu.VMEM((order, order), F32),

time: 79.5 us -> 78.4 us (0.986)
  Pallas kernels: 77.1 us -> 75.9 us
    pallas_call x1, Pallas kernels: 77.1 us -> 75.9 us  [shards(): pl.pallas_call(functools.partial(kernel, n_arc, n_par), out_shape=jax.Sha...]
where the time goes in v5:
time: 78.4 us; the launch traced here: 78.2 us
  Pallas kernels  75.9 us (97%)
  local copies, waits for them, and re-layouts  2.27 us (3%)
    pallas_call x1, Pallas kernels, shards(): pl.pallas_call(functools.partial(kernel, n_arc, n_par), out_shape=jax.Sha...  75.9 us
    unnamed x1, local copies, waits for them, and re-layouts  2.27 us

profile of v5, /device:TPU:1, one launch (start us, length us, event | category | flops | bytes accessed | tf_op | source)
XLA Modules:
  0.0 78.2 jit_solution(11631949418393173666)
XLA Ops:
  0.0 75.9 %info_rows.1 = f32[64,4096]{1,0:T(8,128)} custom-call(f32[256,4096]{1,0:T(8,128)} %obs_hbm.1, s32[2,32]{1,0:T(2,128)} %mask_hbm.1, s32[2]{0:T(128)} %owner_hbm.1), custom_call_target="tpu_custom_call" | custom-call | tf_op jit(solution)/shard_map/info_rows/pallas_call | solution.py:391
  75.9 2.3 %copy.5 = f32[64,4096]{1,0:T(8,128)} copy(f32[64,4096]{1,0:T(8,128)} %info_rows.1) | data formatting | bytes 2097152

commit v6 on v5

--- a/solution.py
+++ b/solution.py
@@ -244,8 +244,6 @@
         stack_ref[:, at:at + 3 * rows] = jnp.concatenate([high, high, low], 1)
 
     fill_stack(0, turned)
-    sibling_panel_copy().wait_recv()
-    fill_stack(3 * rows, in_order(other_panel_ref).T)
 
     def owner_chip(t):
         side = t % 2
@@ -261,21 +259,27 @@
     def column_of(t):
         return pl.multiple_of(((t % 2) * 4 + owner_chip(t)) * width, BLK)
 
-    def cross_tile(t):
-        own = obs_ref[:, pl.ds(pl.multiple_of(core * (cols // 2) + column_of(t), BLK), width)]
-        theirs = other_obs_ref[:, pl.ds(column_of(t), width)]
-        up, down = halves(own)
-        their_up, their_down = halves(theirs)
-        stacked = jnp.concatenate([up, down, up, their_up, their_down, their_up], 0)
-        return jnp.dot(stack_ref[...], stacked, preferred_element_type=F32)
+    def product(at, columns):
+        up, down = halves(columns)
+        return jnp.dot(stack_ref[:, at:at + 3 * rows], jnp.concatenate([up, down, up], 0), preferred_element_type=F32)
+
+    def own_product(t):
+        return product(0, obs_ref[:, pl.ds(pl.multiple_of(core * (cols // 2) + column_of(t), BLK), width)])
+
+    def other_product(t):
+        return product(3 * rows, other_obs_ref[:, pl.ds(column_of(t), width)])
 
     def one_copy(t):
         to = (chip + 1 - 2 * (chip % 2)) if t % 2 == 0 else (chips - 1 - chip)
         return send(sums_ref.at[t], from_one_ref.at[t], one_sems, t, {"arc": 2 * to + core})
 
+    for t in range(4):
+        sums_ref[t] = own_product(t)
     obs_copy().wait_recv()
+    sibling_panel_copy().wait_recv()
+    fill_stack(3 * rows, in_order(other_panel_ref).T)
     for t in range(4):
-        sums_ref[t] = cross_tile(t)
+        sums_ref[t] = sums_ref[t] + other_product(t)
         one_copy(t).start()
 
     each(n_arc - 1, lambda i: gram_copy(i).wait_recv())
@@ -296,7 +300,7 @@
     each(n_par - 1, lambda i: all_copy(i).start())
 
     for t in range(4, 8):
-        sums_ref[t] = cross_tile(t)
+        sums_ref[t] = own_product(t) + other_product(t)
 
     all_all().wait_recv()
     fwd = send(gram_all_ref.at[:, core], gram_all_ref.at[:, core], core_sems, 2, sibling)

time: 78.4 us -> 77.9 us (level)
  no operation moved by 1% of the time
where the time goes in v6:
time: 77.9 us; the launch traced here: 77.8 us
  Pallas kernels  75.5 us (97%)
  local copies, waits for them, and re-layouts  2.27 us (3%)
    pallas_call x1, Pallas kernels, shards(): pl.pallas_call(functools.partial(kernel, n_arc, n_par), out_shape=jax.Sha...  75.5 us
    unnamed x1, local copies, waits for them, and re-layouts  2.27 us

profile of v6, /device:TPU:1, one launch (start us, length us, event | category | flops | bytes accessed | tf_op | source)
XLA Modules:
  0.0 77.8 jit_solution(6040701527854342632)
XLA Ops:
  0.0 75.5 %info_rows.1 = f32[64,4096]{1,0:T(8,128)} custom-call(f32[256,4096]{1,0:T(8,128)} %obs_hbm.1, s32[2,32]{1,0:T(2,128)} %mask_hbm.1, s32[2]{0:T(128)} %owner_hbm.1), custom_call_target="tpu_custom_call" | custom-call | tf_op jit(solution)/shard_map/info_rows/pallas_call | solution.py:395
  75.5 2.3 %copy.5 = f32[64,4096]{1,0:T(8,128)} copy(f32[64,4096]{1,0:T(8,128)} %info_rows.1) | data formatting | bytes 2097152

commit v7 on v6

--- a/solution.py
+++ b/solution.py
@@ -86,7 +86,7 @@
     n_arc, n_par,
     obs_hbm, mask_hbm, owner_hbm, out_ref,
     obs_ref, mask_ref, owner_ref,
-    part_ref, piece_ref, panel_ref, other_obs_ref, other_panel_ref, turned_ref, stack_ref,
+    part_ref, piece_ref, panel_ref, other_obs_ref, other_turned_ref, turned_ref, stack_ref,
     gram_ref, gram_piece_ref, gram_all_ref, fac_ref,
     sums_ref, from_one_ref, from_two_ref, result_ref,
     load_sems, part_sems, panel_sems, gram_sems, all_sems, core_sems, one_sems, two_sems, out_sems,
@@ -172,8 +172,8 @@
         there = pl.ds(pl.multiple_of((1 - core) * (cols // 2), BLK), cols // 2)
         return send(obs_ref.at[:, there], other_obs_ref, core_sems, 0, sibling)
 
-    def sibling_panel_copy():
-        return send(panel_ref, other_panel_ref, core_sems, 1, sibling)
+    def sibling_turned_copy():
+        return send(turned_ref, other_turned_ref, core_sems, 1, sibling)
 
     owns_last = par == n_par - 1
     own_share = share_of(par)
@@ -215,7 +215,6 @@
 
     each(n_par - 1, lambda i: panel_copy(i).start())
     panel_all().wait_recv()
-    sibling_panel_copy().start()
 
     def in_order(ref):
         one, two = ref[:, :PANEL], ref[:, PANEL:]
@@ -224,6 +223,7 @@
     panel = in_order(panel_ref)
     turned = panel.T
     turned_ref[...] = turned
+    sibling_turned_copy().start()
     band_rows = TILE // n_par
     picked = [turned_ref[pl.ds(pl.multiple_of(i * TILE + par * band_rows, 8), band_rows), :] for i in range(tiles)]
     gram_rows = dot_nn(jnp.concatenate(picked, 0), panel)
@@ -273,13 +273,14 @@
         to = (chip + 1 - 2 * (chip % 2)) if t % 2 == 0 else (chips - 1 - chip)
         return send(sums_ref.at[t], from_one_ref.at[t], one_sems, t, {"arc": 2 * to + core})
 
-    for t in range(4):
+    for t in range(2):
         sums_ref[t] = own_product(t)
     obs_copy().wait_recv()
-    sibling_panel_copy().wait_recv()
-    fill_stack(3 * rows, in_order(other_panel_ref).T)
+    sibling_turned_copy().wait_recv()
+    fill_stack(3 * rows, other_turned_ref[...])
     for t in range(4):
-        sums_ref[t] = sums_ref[t] + other_product(t)
+        own = sums_ref[t] if t < 2 else own_product(t)
+        sums_ref[t] = own + other_product(t)
         one_copy(t).start()
 
     each(n_arc - 1, lambda i: gram_copy(i).wait_recv())
@@ -370,7 +371,7 @@
     all_all().wait_send()
     fwd.wait_send()
     obs_copy().wait_send()
-    sibling_panel_copy().wait_send()
+    sibling_turned_copy().wait_send()
 
     for t in range(4):
         one_copy(t).wait_send()
@@ -405,7 +406,7 @@
             pltpu.VMEM((n_par - 1, share, order), F32),
             pltpu.VMEM((rows, order), F32),
             pltpu.VMEM((rows, cols // 2), F32),
-            pltpu.VMEM((rows, order), F32),
+            pltpu.VMEM((order, rows), F32),
             pltpu.VMEM((order, rows), F32),
             pltpu.VMEM((order, 6 * rows), BF16),
             pltpu.VMEM((2 * slice_rows, TILE), F32),

time: 77.9 us -> 77.9 us (level)
  no operation moved by 1% of the time
where the time goes in v7:
time: 77.9 us; the launch traced here: 77.7 us
  Pallas kernels  75.4 us (97%)
  local copies, waits for them, and re-layouts  2.27 us (3%)
    pallas_call x1, Pallas kernels, shards(): pl.pallas_call(functools.partial(kernel, n_arc, n_par), out_shape=jax.Sha...  75.4 us
    unnamed x1, local copies, waits for them, and re-layouts  2.27 us

profile of v7, /device:TPU:1, one launch (start us, length us, event | category | flops | bytes accessed | tf_op | source)
XLA Modules:
  0.0 77.7 jit_solution(12513643326756627088)
XLA Ops:
  0.0 75.4 %info_rows.1 = f32[64,4096]{1,0:T(8,128)} custom-call(f32[256,4096]{1,0:T(8,128)} %obs_hbm.1, s32[2,32]{1,0:T(2,128)} %mask_hbm.1, s32[2]{0:T(128)} %owner_hbm.1), custom_call_target="tpu_custom_call" | custom-call | tf_op jit(solution)/shard_map/info_rows/pallas_call | solution.py:396
  75.5 2.3 %copy.5 = f32[64,4096]{1,0:T(8,128)} copy(f32[64,4096]{1,0:T(8,128)} %info_rows.1) | data formatting | bytes 2097152

commit v8 on v6

--- a/solution.py
+++ b/solution.py
@@ -325,7 +325,7 @@
 
     for k in range(tiles):
         factor_step(fac_ref, k, tiles)
-        if k == 1:
+        if k == 0:
             for t in range(2):
                 one_copy(t).wait_recv()
                 sums_ref[4 + t] = sums_ref[4 + t] + from_one_ref[t]

time: 77.9 us -> 77.9 us (level)
  no operation moved by 1% of the time
where the time goes in v8:
time: 77.9 us; the launch traced here: 77.8 us
  Pallas kernels  75.5 us (97%)
  local copies, waits for them, and re-layouts  2.27 us (3%)
    pallas_call x1, Pallas kernels, shards(): pl.pallas_call(functools.partial(kernel, n_arc, n_par), out_shape=jax.Sha...  75.5 us
    unnamed x1, local copies, waits for them, and re-layouts  2.27 us

profile of v8, /device:TPU:1, one launch (start us, length us, event | category | flops | bytes accessed | tf_op | source)
XLA Modules:
  0.0 77.8 jit_solution(4350961840032752341)
XLA Ops:
  0.0 75.5 %info_rows.1 = f32[64,4096]{1,0:T(8,128)} custom-call(f32[256,4096]{1,0:T(8,128)} %obs_hbm.1, s32[2,32]{1,0:T(2,128)} %mask_hbm.1, s32[2]{0:T(128)} %owner_hbm.1), custom_call_target="tpu_custom_call" | custom-call | tf_op jit(solution)/shard_map/info_rows/pallas_call | solution.py:395
  75.5 2.3 %copy.5 = f32[64,4096]{1,0:T(8,128)} copy(f32[64,4096]{1,0:T(8,128)} %info_rows.1) | data formatting | bytes 2097152
